TPU v7x, 32 devices: a whole 2x2x4 slice. The times are simulated.
32 devices in a mesh: seq: 16 (over z, y, x), tp: 2 (over core).
Axes of the slice: x: 2, y: 2, z: 4, core: 2. Of those that a mesh axis runs over, the one named last changes fastest.
Arguments:
- hidden: bfloat16 [4096, 1024], P('seq'), may hold values from -6 to 6
- norm1_gain: float32 [1024], replicated, may hold values from 0.25 to 1.75
- w_query: bfloat16 [1024, 256], P(None, 'tp'), may hold values from -3 to 3
- w_key: bfloat16 [1024, 128], P(None, 'tp'), may hold values from -2 to 2
- w_value: bfloat16 [1024, 128], P(None, 'tp'), may hold values from -0.1875 to 0.1875
- w_out: bfloat16 [256, 1024], P('tp'), may hold values from -0.375 to 0.375
- norm2_gain: float32 [1024], replicated, may hold values from 0.25 to 1.75
- w_gate: bfloat16 [16, 1024, 512], P('seq'), may hold values from -0.1875 to 0.1875
- w_up: bfloat16 [16, 1024, 512], P('seq'), may hold values from -0.1875 to 0.1875
- w_down: bfloat16 [16, 512, 1024], P('seq'), may hold values from -0.25 to 0.25
- cache_in: bfloat16 [144, 256, 2, 128], P('seq', None, 'tp'), may hold values from -48 to 48
- cache_len: int32 [2], replicated, may hold values from 0 to 16384, as said below
- block_table: int32 [144], replicated, may hold values from 0 to 143, each once
- routes: int32 [4096, 8], P(('seq', 'tp')), may hold values from 0 to 15, all different within a row; in each aligned block of 128 rows (0 to 127, 128 to 255, ...) at most 96 rows name the same one
- gate_w: float32 [4096, 8], P(('seq', 'tp')), may hold values from 0.05 to 0.35
Outputs:
- hidden_out: bfloat16 [4096, 1024], P(('seq', 'tp'))
- cache_out: bfloat16 [144, 256, 2, 128], P('seq', None, 'tp')
Inputs may be any that keep to these rules, and one draw needn't show every extreme that they name: `cache_len`: some request holds exactly 16384 entries. `block_table`: each pool block appears once; pool block b lies on index b // 9 of seq. `routes`: each row names 8 different experts; among the rows of one device (aligned blocks of 128 rows) no expert is named more than 96 times, a bound that some block reaches.
All inputs are finite; a program needn't handle non-finite values.
Results may differ from a plain program's by a relative error of at most 0.035.
The roundings to bfloat16 on the way count: a program that leaves them out, or rounds other values in their place, can miss the bound.
Values may be sent and summed in bfloat16 or wider, within the bound.
A program may use at most 128 MiB of HBM per device.

v0:
```python
import math

import jax
import jax.numpy as jnp
from jax import lax
from jax.sharding import PartitionSpec as P

D = 1024
HD = 64
GROUP = 2
TOP = 8
STRETCH = 2048
BS = 256
TOK_DEV = 256
MAXB = 72


norm_eps = 1e-05
rope_base = 10000.0
mask_fill = -1e30


def rms_scale(inputs, gains):
    floats = inputs.astype(jnp.float32)
    mean_square = jnp.mean(floats * floats, axis=-1, keepdims=True)
    return (floats * lax.rsqrt(mean_square + norm_eps) * gains).astype(jnp.bfloat16)


def rotate(vectors, positions):
    halfway = vectors.shape[-1] // 2
    counter = jnp.arange(halfway, dtype=jnp.int32).astype(jnp.float32)
    frequency = jnp.exp(counter * (-2.0 * math.log(rope_base) / vectors.shape[-1]))
    angles = positions.astype(jnp.float32)[:, None] * frequency[None, :]
    cosine = jnp.cos(angles)[:, None, :]
    sine_part = jnp.sin(angles)[:, None, :]
    front_half = vectors[..., :halfway]
    back_half = vectors[..., halfway:]
    return jnp.concatenate(
        [front_half * cosine - back_half * sine_part, back_half * cosine + front_half * sine_part],
        axis=-1,
    )


def on_device(
    hidden,
    norm1_gain,
    w_query,
    w_key,
    w_value,
    w_out,
    norm2_gain,
    w_gate,
    w_up,
    w_down,
    cache_in,
    cache_len,
    block_table,
    routes,
    gate_w,
):
    seq_count = lax.axis_size("seq")
    seq_place = lax.axis_index("seq")
    tp_place = lax.axis_index("tp")
    scaling = 1.0 / math.sqrt(HD)
    token_ids = seq_place * TOK_DEV + jnp.arange(TOK_DEV, dtype=jnp.int32)
    offsets = token_ids % STRETCH
    positions = cache_len[token_ids // STRETCH] + offsets
    normed = rms_scale(hidden, norm1_gain)
    queries = jnp.dot(normed, w_query, preferred_element_type=jnp.float32).reshape(
        TOK_DEV, GROUP, HD
    )
    queries = rotate(queries, positions).astype(jnp.bfloat16)
    key_rows = jnp.dot(normed, w_key, preferred_element_type=jnp.float32).reshape(TOK_DEV, 1, HD)
    key_rows = rotate(key_rows, positions).reshape(TOK_DEV, HD).astype(jnp.bfloat16)
    value_rows = jnp.dot(normed, w_value, preferred_element_type=jnp.float32).astype(jnp.bfloat16)
    new_rows = jnp.concatenate([key_rows, value_rows], axis=1)
    flat_queries = queries.reshape(TOK_DEV, GROUP * HD)
    all_queries, all_rows = (
        lax.all_gather(flat_queries, "seq", axis=0, tiled=True),
        lax.all_gather(new_rows, "seq", axis=0, tiled=True),
    )
    query_total = all_queries.shape[0]
    blk_count = cache_in.shape[0]
    pool_size = block_table.shape[0]
    pool_ids = seq_place * blk_count + jnp.arange(blk_count, dtype=jnp.int32)
    matched = block_table[None, :] == pool_ids[:, None]
    slot_of = jnp.sum(
        jnp.where(matched, jnp.arange(pool_size, dtype=jnp.int32)[None, :], 0), axis=1
    )
    block_req = slot_of // MAXB
    block_pos = slot_of % MAXB * BS
    cache_layer = cache_in[:, :, 0, :]
    span_rows = STRETCH * GROUP

    def update(block_id, states):
        row_peak, row_mass, row_accum = states
        request = block_req[block_id]
        first_row = request * span_rows
        filled = cache_len[request]
        entries = cache_layer[block_id]
        span_queries = lax.dynamic_slice_in_dim(all_queries, request * STRETCH, STRETCH, 0).reshape(
            span_rows, HD
        )
        scores = (
            jnp.einsum(
                "qd,kd->qk", span_queries, entries[:, :HD], preferred_element_type=jnp.float32
            )
            * scaling
        )
        visible = block_pos[block_id] + jnp.arange(BS, dtype=jnp.int32) < filled
        scores = jnp.where(visible[None, :], scores, mask_fill)
        old_peak = lax.dynamic_slice_in_dim(row_peak, first_row, span_rows, 0)
        new_peak = jnp.maximum(old_peak, jnp.max(scores, axis=-1))
        weights = jnp.where(visible[None, :], jnp.exp(scores - new_peak[:, None]), 0.0)
        retain = jnp.exp(old_peak - new_peak)
        old_mass = lax.dynamic_slice_in_dim(row_mass, first_row, span_rows, 0)
        old_accum = lax.dynamic_slice_in_dim(row_accum, first_row, span_rows, 0)
        mixed = jnp.einsum(
            "qk,kd->qd",
            weights.astype(jnp.bfloat16),
            entries[:, HD:],
            preferred_element_type=jnp.float32,
        )
        row_peak = lax.dynamic_update_slice_in_dim(row_peak, new_peak, first_row, 0)
        row_mass = lax.dynamic_update_slice_in_dim(
            row_mass, old_mass * retain + jnp.sum(weights, axis=-1), first_row, 0
        )
        row_accum = lax.dynamic_update_slice_in_dim(
            row_accum, old_accum * retain[:, None] + mixed, first_row, 0
        )
        return (row_peak, row_mass, row_accum)

    def visit_block(block_id, states):
        return update(block_id, states)

    flat_total = query_total * GROUP
    start_states = (
        jnp.full((flat_total,), mask_fill, jnp.float32),
        jnp.zeros((flat_total,), jnp.float32),
        jnp.zeros((flat_total, HD), jnp.float32),
    )
    row_peak, row_mass, row_accum = lax.fori_loop(0, blk_count, visit_block, start_states)
    each_peak, each_mass, each_accum = (
        lax.all_to_all(
            row_peak.reshape(seq_count, TOK_DEV * GROUP),
            "seq",
            split_axis=0,
            concat_axis=0,
            tiled=True,
        ),
        lax.all_to_all(
            row_mass.reshape(seq_count, TOK_DEV * GROUP),
            "seq",
            split_axis=0,
            concat_axis=0,
            tiled=True,
        ),
        lax.all_to_all(
            row_accum.reshape(seq_count, TOK_DEV, GROUP * HD),
            "seq",
            split_axis=0,
            concat_axis=0,
            tiled=True,
        ),
    )
    top_peak = jnp.max(each_peak, axis=0)
    factor = jnp.exp(each_peak - top_peak[None])
    got_mass = jnp.sum(each_mass * factor, axis=0).reshape(TOK_DEV, GROUP)
    got_accum = jnp.sum(
        each_accum.reshape(seq_count, TOK_DEV * GROUP, HD) * factor[..., None], axis=0
    ).reshape(TOK_DEV, GROUP, HD)
    my_peak = top_peak.reshape(TOK_DEV, GROUP)
    own_request = seq_place * TOK_DEV // STRETCH
    own_rows = lax.dynamic_slice_in_dim(all_rows, own_request * STRETCH, STRETCH, 0)
    own_queries = queries.reshape(TOK_DEV * GROUP, HD)
    self_scores = (
        jnp.einsum("qd,kd->qk", own_queries, own_rows[:, :HD], preferred_element_type=jnp.float32)
        * scaling
    )
    row_offsets = jnp.repeat(offsets, GROUP)
    causal = jnp.arange(STRETCH, dtype=jnp.int32)[None, :] <= row_offsets[:, None]
    self_scores = jnp.where(causal, self_scores, mask_fill)
    self_peak = jnp.max(self_scores, axis=-1)
    self_weights = jnp.where(causal, jnp.exp(self_scores - self_peak[:, None]), 0.0)
    self_mass = jnp.sum(self_weights, axis=-1).reshape(TOK_DEV, GROUP)
    self_accum = jnp.einsum(
        "qk,kd->qd",
        self_weights.astype(jnp.bfloat16),
        own_rows[:, HD:],
        preferred_element_type=jnp.float32,
    ).reshape(TOK_DEV, GROUP, HD)
    self_peak = self_peak.reshape(TOK_DEV, GROUP)
    final_peak = jnp.maximum(my_peak, self_peak)
    cache_share = jnp.exp(my_peak - final_peak)
    self_share = jnp.exp(self_peak - final_peak)
    denom = got_mass * cache_share + self_mass * self_share
    attention = (got_accum * cache_share[..., None] + self_accum * self_share[..., None]) / denom[
        ..., None
    ]
    attention = attention.reshape(TOK_DEV, GROUP * HD).astype(jnp.bfloat16)
    tp_rows = TOK_DEV // lax.axis_size("tp")
    head_total = lax.psum_scatter(
        jnp.dot(attention, w_out, preferred_element_type=jnp.float32).astype(jnp.bfloat16),
        "tp",
        scatter_dimension=0,
        tiled=True,
    ).astype(jnp.float32)
    own_hidden = lax.dynamic_slice_in_dim(hidden, tp_place * tp_rows, tp_rows, 0)
    residual = (own_hidden.astype(jnp.float32) + head_total).astype(jnp.bfloat16)
    normed2 = rms_scale(residual, norm2_gain)
    capacity = min(tp_rows, 3 * tp_rows * TOP // (2 * seq_count))
    flat_expert = routes.reshape(tp_rows * TOP)
    onehot = (flat_expert[:, None] == jnp.arange(seq_count, dtype=jnp.int32)[None, :]).astype(
        jnp.int32
    )
    ranking = jnp.sum((jnp.cumsum(onehot, axis=0) - onehot) * onehot, axis=1)
    slot_ids = flat_expert * capacity + ranking
    sources = jnp.arange(tp_rows * TOP, dtype=jnp.int32) // TOP
    table = jnp.zeros((seq_count * capacity,), jnp.int32).at[slot_ids].set(sources)
    occupied = jnp.zeros((seq_count * capacity,), jnp.bool_).at[slot_ids].set(True)
    outgoing = jnp.where(occupied[:, None], normed2[table], jnp.zeros((), jnp.bfloat16)).reshape(
        seq_count, capacity, D
    )
    incoming = lax.all_to_all(outgoing, "seq", split_axis=0, concat_axis=0, tiled=True)
    senders = incoming.shape[0]
    items = incoming.shape[1]
    flat_rows = incoming.reshape(senders * items, D)
    gate_part = jnp.dot(flat_rows, w_gate[0], preferred_element_type=jnp.float32)
    up_part = jnp.dot(flat_rows, w_up[0], preferred_element_type=jnp.float32)
    inner = (jax.nn.silu(gate_part) * up_part).astype(jnp.bfloat16)
    answer = jnp.dot(inner, w_down[0], preferred_element_type=jnp.float32).astype(jnp.bfloat16)
    answered = answer.reshape(senders, items, D)
    returned = lax.all_to_all(answered, "seq", split_axis=0, concat_axis=0, tiled=True)
    picked = returned.reshape(seq_count * capacity, D)[slot_ids].reshape(tp_rows, TOP, D)
    expert_sum = jnp.sum(gate_w[..., None] * picked.astype(jnp.float32), axis=1)
    hidden_out = (residual.astype(jnp.float32) + expert_sum).astype(jnp.bfloat16)
    block_offsets = block_pos[:, None] + jnp.arange(BS, dtype=jnp.int32)[None, :]
    block_fill = cache_len[block_req][:, None]
    inside = (block_offsets >= block_fill) & (block_offsets < block_fill + STRETCH)
    source_rows = block_req[:, None] * STRETCH + jnp.clip(
        block_offsets - block_fill, 0, STRETCH - 1
    )
    fresh = all_rows[source_rows]
    cache_out = jnp.where(inside[..., None], fresh, cache_layer)[:, :, None, :]
    return (hidden_out, cache_out)


def solution(mesh):
    placed = (
        P("seq", None),
        P(),
        P(None, "tp"),
        P(None, "tp"),
        P(None, "tp"),
        P("tp", None),
        P(),
        P("seq", None, None),
        P("seq", None, None),
        P("seq", None, None),
        P("seq", None, "tp", None),
        P(),
        P(),
        P(("seq", "tp"), None),
        P(("seq", "tp"), None),
    )
    return jax.shard_map(
        on_device,
        mesh=mesh,
        in_specs=placed,
        out_specs=(P(("seq", "tp"), None), P("seq", None, "tp", None)),
        check_vma=False,
    )
```

profile of v0, /device:TPU:0, one launch (start us, length us, event | category | flops | bytes accessed | tf_op | source)
XLA Modules:
  0.0 586.2 jit_solution(10715050601023402985)
XLA Ops:
  15.0 56.5 %all-gather.3.cloned.1.call-done = bf16[4096,128]{0,1:T(8,128)(2,1)} async-done(((bf16[256,128]{0,1:T(8,128)(2,1)}), bf16[4096,128]{0,1:T(8,128)(2,1)}) %all-gather.3.cloned.1.call-update) | async-done | bytes 1048592 | tf_op jit(solution)/shard_map/all_gather | solution.py:79
  74.3 189.7 %while.17 = (s32[]{:T(128)}, f32[8192]{0:T(1024)}, f32[8192]{0:T(1024)}, f32[8192,64]{0,1:T(8,128)}, s32[9]{0:T(128)S(1)}, /*index=5*/s32[9]{0:T(128)S(1)}, s32[...) while((s32[]{:T(128)}, f32[8192]{0:T(1024)}, ...), condition=%wide.region_5.6_spmd, body=%wide.region_2.5_spmd.sunk | while | flops 278405632 | bytes 35767656 | solution.py:142
  87.0 3.2 fusion.100
  91.6 3.1 fusion.101
  103.8 2.7 fusion.98
  108.1 3.2 fusion.100
  112.7 3.1 fusion.101
  124.9 2.7 fusion.98
  129.2 3.2 fusion.100
  133.8 3.1 fusion.101
  146.0 2.7 fusion.98
  150.3 3.2 fusion.100
  154.9 3.1 fusion.101
  167.1 2.7 fusion.98
  171.4 3.2 fusion.100
  175.9 3.1 fusion.101
  188.1 2.7 fusion.98
  192.4 3.2 fusion.100
  197.0 3.1 fusion.101
  213.5 3.2 fusion.100
  218.1 3.1 fusion.101
  234.5 3.2 fusion.100
  239.1 3.1 fusion.101
  251.3 2.7 fusion.98
  255.6 3.2 fusion.100
  260.2 3.1 fusion.101
  263.9 4.4 all-to-all-start.1
  268.7 7.0 %all-to-all-done.1 = f32[16,1,512]{2,1,0:T(1,128)S(1)} async-done(((f32[16,1,512]{2,1,0:T(1,128)}), f32[16,1,512]{2,1,0:T(1,128)S(1)}, u32[]{:S(2)}, u32[]{:S(2)}) %all-to-all-start.1) | async-done | bytes 32800 | tf_op jit(solution)/shard_map/all_to_all | solution.py:144
  275.7 3.5 all-to-all-start.2
  280.5 3.8 copy.79
  284.3 4.6 reshape.606
  288.9 6.9 %all-to-all-start = ((f32[16,256,128]{2,1,0:T(8,128)}), f32[16,256,128]{2,1,0:T(8,128)}, u32[]{:S(2)}, u32[]{:S(2)}) async-start(f32[16,256,128]{2,1,0:T(8,128)} %reshape.606), calls=%async_computation | async-start | bytes 4194304 | tf_op jit(solution)/shard_map/all_to_all | solution.py:158
  297.7 66.4 %all-gather.5.cloned.1.call-done = bf16[4096,128]{0,1:T(8,128)(2,1)} async-done(((bf16[256,128]{0,1:T(8,128)(2,1)}), bf16[4096,128]{0,1:T(8,128)(2,1)}) %all-gather.5.cloned.1.call-update) | async-done | bytes 1048592 | tf_op jit(solution)/shard_map/all_gather | solution.py:80
  364.1 3.8 fusion.12
  368.1 3.4 fusion.16
  372.3 3.5 fusion.14
  379.5 3.3 mul.313
  393.2 4.5 reduce-window.6
  398.4 4.3 scatter_custom_fusion.1
  402.7 4.6 scatter_custom_fusion
  408.8 5.8 gather_fusion
  416.7 75.3 %all_to_all.39 = bf16[16,96,1024]{2,1,0:T(8,128)(2,1)S(1)} all-to-all(bf16[16,96,1024]{2,1,0:T(8,128)(2,1)S(1)} %broadcast_select_fusion), channel_id=1, replica_groups=mesh['seq'=16,'tp'=2] {'seq'}, dimensions={0} | all-to-all | bytes 6291456 | tf_op jit(solution)/shard_map/all_to_all | solution.py:224
  493.7 3.5 fusion.24
  497.2 8.3 %convolution_convert_fusion = bf16[1536,1024]{1,0:T(8,128)(2,1)} fusion(bf16[1536,1024]{1,0:T(8,128)(2,1)} %bitcast.105, f32[1536,512]{1,0:T(8,128)} %fusion.24, bf16[1,512,1024]{2,1,0:T(8,128)(2,1)S(1)} %copy-done, bf16[1,1024,512]{2,1,0:T(8,128)(2,1)S(1)} %copy-done.21), kind=kOutput, calls=%fused_computation.30 | convolution fusion | flops 3227516928 | bytes 11534336 | tf_op jit(solution)/shard_map/dot_general | solution.py:231
  505.5 4.6 all-to-all-start.4
  511.9 4.7 gather_fusion.3
  518.8 51.6 %all-to-all-done.4 = bf16[16,96,1024]{2,1,0:T(8,128)(2,1)} async-done(((bf16[16,96,1024]{2,1,0:T(8,128)(2,1)}), bf16[16,96,1024]{2,1,0:T(8,128)(2,1)}, u32[]{:S(2)}, u32[]{:S(2)}) %all-to-all-start.4) | async-done | bytes 3145760 | tf_op jit(solution)/shard_map/all_to_all | solution.py:233
  570.3 7.3 %gather_fusion.1 = bf16[1024,1024]{1,0:T(8,128)(2,1)S(1)} fusion(bf16[1536,1024]{1,0:T(8,128)(2,1)} %bitcast.29, s32[1024]{0:T(1024)S(1)} %broadcast_clamp_fusion), kind=kCustom, calls=%fused_computation.1 | custom fusion | bytes 4198400 | tf_op jit(solution)/shard_map/gather | solution.py:234
  (268 shorter events, 126.3 us)
Async XLA Ops:
  7.2 490.1 %copy-start = (bf16[1,512,1024]{2,1,0:T(8,128)(2,1)S(1)}, bf16[1,512,1024]{2,1,0:T(8,128)(2,1)}, u32[]{:S(2)}) copy-start(bf16[1,512,1024]{2,1,0:T(8,128)(2,1)} %param.26) | copy-start | bytes 3145732
  7.2 67.1 %copy-start.2 = (s32[2]{0:T(128)S(1)}, s32[2]{0:T(128)}, u32[]{:S(2)}) copy-start(s32[2]{0:T(128)} %param.28) | copy-start | bytes 28
  7.2 64.3 %all-gather.3.cloned.1.call-start = ((), (), s32[]{:S(2)}) async-start(), calls=%async_computation.6 | async-start | bytes 1114112 | tf_op jit(solution)/shard_map/all_gather | solution.py:79
  14.4 59.8 %copy-start.17 = (s32[9]{0:T(128)}, s32[9]{0:T(128)S(1)}, u32[]{:S(2)}) copy-start(s32[9]{0:T(128)S(1)} %select_reduce_fusion) | copy-start | bytes 112
  74.2 194.1 %copy-start.4 = (bf16[256,1024]{1,0:T(8,128)(2,1)S(1)}, bf16[256,1024]{1,0:T(8,128)(2,1)}, u32[]{:S(2)}) copy-start(bf16[256,1024]{1,0:T(8,128)(2,1)} %param.17) | copy-start | bytes 1572868
  74.2 194.1 %copy-start.22 = (bf16[1024,64]{0,1:T(8,128)(2,1)S(1)}, bf16[1024,64]{0,1:T(8,128)(2,1)}, u32[]{:S(2)}) copy-start(bf16[1024,64]{0,1:T(8,128)(2,1)} %param.21) | copy-start | bytes 393220
  74.2 194.1 %copy-start.23 = (f32[1024]{0:T(1024)S(1)}, f32[1024]{0:T(1024)}, u32[]{:S(2)}) copy-start(f32[1024]{0:T(1024)} %param.18) | copy-start | bytes 12292
  86.1 5.5 copy-start.1
  107.2 5.5 copy-start.1
  128.3 5.5 copy-start.1
  149.4 5.5 copy-start.1
  170.4 5.5 copy-start.1
  191.5 5.5 copy-start.1
  212.6 5.5 copy-start.1
  233.6 5.5 copy-start.1
  254.7 5.5 copy-start.1
  263.9 11.8 %copy-start.12 = (s32[9]{0:T(128)}, s32[9]{0:T(128)S(1)}, u32[]{:S(2)}) copy-start(s32[9]{0:T(128)S(1)} %get-tuple-element.374) | copy-start | bytes 112
  263.9 11.8 %all-to-all-start.1 = ((f32[16,1,512]{2,1,0:T(1,128)}), f32[16,1,512]{2,1,0:T(1,128)S(1)}, u32[]{:S(2)}, u32[]{:S(2)}) async-start(f32[16,1,512]{2,1,0:T(1,128)} %bitcast.10), calls=%async_computation.1 | async-start | bytes 65536 | tf_op jit(solution)/shard_map/all_to_all | solution.py:144
  275.7 13.2 %all-to-all-start.2 = ((f32[16,1,512]{2,1,0:T(1,128)}), f32[16,1,512]{2,1,0:T(1,128)S(1)}, u32[]{:S(2)}, u32[]{:S(2)}) async-start(f32[16,1,512]{2,1,0:T(1,128)} %bitcast.17), calls=%async_computation.2 | async-start | bytes 65536 | tf_op jit(solution)/shard_map/all_to_all | solution.py:151
  284.3 13.2 %copy-start.11 = (s32[128,8]{0,1:T(8,128)S(1)}, s32[128,8]{0,1:T(8,128)}, u32[]{:S(2)}) copy-start(s32[128,8]{0,1:T(8,128)} %param.30) | copy-start | bytes 12292
  288.9 101.0 %all-to-all-start = ((f32[16,256,128]{2,1,0:T(8,128)}), f32[16,256,128]{2,1,0:T(8,128)}, u32[]{:S(2)}, u32[]{:S(2)}) async-start(f32[16,256,128]{2,1,0:T(8,128)} %reshape.606), calls=%async_computation | async-start | bytes 4194304 | tf_op jit(solution)/shard_map/all_to_all | solution.py:158
  295.8 68.3 %all-gather.5.cloned.1.call-start = ((), (), s32[]{:S(2)}) async-start(), calls=%async_computation.7 | async-start | bytes 1114112 | tf_op jit(solution)/shard_map/all_gather | solution.py:80
  296.8 110.6 %reduce-scatter.2.cloned.1.call-start = ((), (), s32[]{:S(2)}) async-start(), calls=%async_computation.8 | async-start | bytes 786432 | tf_op jit(solution)/shard_map/reduce_scatter | solution.py:202
  384.2 7.7 %copy-start.6 = (f32[256,128]{1,0:T(8,128)S(1)}, f32[256,128]{1,0:T(8,128)}, u32[]{:S(2)}) copy-start(f32[256,128]{1,0:T(8,128)} %reshape.610) | copy-start | bytes 393220
  388.4 20.2 %copy-start.14 = (f32[1024]{0:T(1024)S(1)}, f32[1024]{0:T(1024)}, u32[]{:S(2)}) copy-start(f32[1024]{0:T(1024)} %param.23) | copy-start | bytes 12292
  389.9 2.0 copy-start.7
  389.9 2.0 copy-start.8
  389.9 2.0 copy-start.9
  389.9 2.0 copy-start.10
  416.7 77.0 %copy-start.20 = (bf16[1,1024,512]{2,1,0:T(8,128)(2,1)S(1)}, bf16[1,1024,512]{2,1,0:T(8,128)(2,1)}, u32[]{:S(2)}) copy-start(bf16[1,1024,512]{2,1,0:T(8,128)(2,1)} %param.24) | copy-start | bytes 3145732
  492.0 1.7 copy-start.3
  493.7 3.5 copy-start.21
  505.5 4.7 copy-start.15
  505.5 4.8 copy-start.18
  505.5 4.8 copy-start.19
  505.5 5.5 copy-start.13
  505.5 5.5 copy-start.16
  505.5 5.7 copy-start.5
  505.5 64.8 %all-to-all-start.4 = ((bf16[16,96,1024]{2,1,0:T(8,128)(2,1)}), bf16[16,96,1024]{2,1,0:T(8,128)(2,1)}, u32[]{:S(2)}, u32[]{:S(2)}) async-start(bf16[16,96,1024]{2,1,0:T(8,128)(2,1)} %bitcast.103), calls=%async_computation.5 | async-start | bytes 6291456 | tf_op jit(solution)/shard_map/all_to_all | solution.py:233
Sparse Core Ops, SparseCore 0:
  13.7 57.7 all-gather.2
  300.0 64.0 all-gather.4
  393.2 6.7 reduce-scatter.1
where the time goes:
time: 598 us; the launch traced here: 586 us
  waiting for transfers between devices  182 us (30%)
  local copies, waits for them, and re-layouts  111 us (19%)
  other arithmetic  78.1 us (13%)
  blocking collectives  75.3 us (13%)
  matrix products  75.1 us (13%)
  loops' own time  31.2 us (5%)
  starting transfers between devices  19.8 us (3%)
  between operations  14.3 us (2%)
    all_to_all x1, blocking collectives, on_device(): lax.all_to_all(outgoing, 'seq', split_axis=0, concat_axis=0, tiled=True)  75.3 us
    all_gather x1, waiting for transfers between devices, on_device(): lax.all_gather(new_rows, 'seq', axis=0, tiled=True)  66.4 us
    all_gather x1, waiting for transfers between devices, on_device(): lax.all_gather(flat_queries, 'seq', axis=0, tiled=True)  56.5 us
    all_to_all x1, waiting for transfers between devices, on_device(): lax.all_to_all(answered, 'seq', split_axis=0, concat_axis=0, tiled=True)  51.6 us
    another operation x1, loops' own time, on_device(): lax.fori_loop(0, blk_count, visit_block, start_states)  31.2 us
    reduce_sum x9, other arithmetic, update(): jnp.sum(weights, axis=-1)  28.8 us
    dot_general x9, matrix products, update(): jnp.einsum('qk,kd->qd', weights.astype(jnp.bfloat16), entries[:, HD:], pr...  28 us
    dot_general x9, matrix products, update(): jnp.einsum('qd,kd->qk', span_queries, entries[:, :HD], preferred_element_...  23.9 us
  transfers between devices with their start and end apart: 7, of which 4 were waited for; matrix products, arithmetic and copies ran while one was open for 10% of the time, Pallas kernels for 0%

commit v1 on v0

v1 whole, which is shorter than its diff:
```python
import functools
import math

import jax
import jax.numpy as jnp
from jax import lax
from jax.experimental import pallas as pl
from jax.experimental.pallas import tpu as pltpu
from jax.sharding import PartitionSpec as P

D = 1024
HD = 64
GROUP = 2
STRETCH = 2048
BS = 256
TOK_DEV = 256
MAXB = 72
SPAN = STRETCH // TOK_DEV

norm_eps = 1e-05
rope_base = 10000.0
mask_fill = -1e30
MESH = pl.DeviceIdType.MESH
F32 = jnp.float32
BF16 = jnp.bfloat16


def bit_orders(bits, count):
    low = list(range(bits - 1))
    orders = []
    for part in range(count):
        turn = part % max(1, len(low))
        orders.append([bits - 1] + low[turn:] + low[:turn])
    return orders


def flip(place, rel, bits):
    out = place
    for bit in range(bits):
        if rel >> bit & 1:
            out = out + (1 - 2 * (place // (1 << bit) % 2)) * (1 << bit)
    return out


def slot_in(order, place, other):
    out = 0
    for step, bit in enumerate(order):
        out = out + (place // (1 << bit) + other // (1 << bit)) % 2 * (1 << step)
    return out


def rel_of(order, slot):
    return sum(1 << bit for step, bit in enumerate(order) if slot >> step & 1)


def row_parts(rows):
    units = rows // 16
    count = min(3, units)
    sizes = [(units // count + (1 if i < units % count else 0)) * 16 for i in range(count)]
    return [(sum(sizes[:i]), size) for i, size in enumerate(sizes)]


def scaled(floats, gains):
    mean_square = jnp.mean(floats * floats, axis=-1, keepdims=True)
    return (floats * lax.rsqrt(mean_square + norm_eps) * gains).astype(BF16)


def project_kernel(bits, hidden, gain, wq, wkv, cosine, sine, buf, send, recv):
    me, tp = lax.axis_index("seq"), lax.axis_index("tp")
    barrier = pltpu.get_barrier_semaphore()
    for bit in range(bits):
        pl.semaphore_signal(
            barrier, inc=1, device_id=(flip(me, 1 << bit, bits), tp), device_id_type=MESH
        )
    normed = scaled(hidden[...].astype(F32), gain[...])
    cos, sin = cosine[...], sine[...]

    def turned(rows):
        a, b = rows[:32], rows[32:]
        return jnp.concatenate([a * cos - b * sin, b * cos + a * sin], axis=0)

    q = jnp.dot(normed, wq[...], preferred_element_type=F32).T
    kv = jnp.dot(normed, wkv[...], preferred_element_type=F32).T
    buf[0, 0] = (turned(q[:HD]) * 0.125).astype(BF16)
    buf[1, 0] = (turned(q[HD:]) * 0.125).astype(BF16)
    buf[2, 0] = turned(kv[:HD]).astype(BF16)
    buf[3, 0] = kv[HD:].astype(BF16)
    pl.semaphore_wait(barrier, bits)
    orders = bit_orders(bits, 4)
    copies = {}
    for step in range(bits):
        size = 1 << step
        for part in range(4):
            if step:
                copies[part, step - 1].wait_recv()
            copy = pltpu.make_async_remote_copy(
                src_ref=buf.at[part, pl.ds(0, size)],
                dst_ref=buf.at[part, pl.ds(size, size)],
                send_sem=send.at[part, step],
                recv_sem=recv.at[part, step],
                device_id=(flip(me, 1 << orders[part][step], bits), tp),
                device_id_type=MESH,
            )
            copy.start()
            copies[part, step] = copy
    for part in range(4):
        copies[part, bits - 1].wait_recv()
    for copy in copies.values():
        copy.wait_send()


CHUNK = 4


def cache_kernel(
    bits, slots, lens, buf, cache, gates, acc_out, stat_out, cache_out, vt, peak, mass, accum
):
    me = lax.axis_index("seq")
    seq_count = 1 << bits
    blocks = cache.shape[0]
    orders = bit_orders(bits, 4)

    def place_block(b, carry):
        slot = slots[b]
        request = slot // MAXB
        shift = slot % MAXB * BS - lens[request]
        vt[b] = cache[b][:, HD:].astype(F32).T.astype(BF16)
        cache_out[b] = cache[b]

        @pl.when((shift > -BS) & (shift < STRETCH))
        def _():
            first = (shift + STRETCH) // TOK_DEV - SPAN
            entry = lax.broadcasted_iota(jnp.int32, (BS, TOK_DEV), 0)
            token = lax.broadcasted_iota(jnp.int32, (BS, TOK_DEV), 1)
            keys = jnp.zeros((BS, HD), F32)
            values = jnp.zeros((BS, HD), F32)
            for extra in range(2):
                window = first + extra
                held = request * SPAN + jnp.clip(window, 0, SPAN - 1)
                hit = (entry + (shift - window * TOK_DEV) == token) & (window >= 0) & (
                    window < SPAN
                )
                pick = jnp.where(hit, 1.0, 0.0).astype(BF16)
                dims = (((1,), (1,)), ((), ()))
                keys += lax.dot_general(
                    pick, buf[2, slot_in(orders[2], me, held)], dims, preferred_element_type=F32
                )
                values += lax.dot_general(
                    pick, buf[3, slot_in(orders[3], me, held)], dims, preferred_element_type=F32
                )
            row = lax.broadcasted_iota(jnp.int32, (BS, 2 * HD), 0) + shift
            fresh = jnp.concatenate([keys, values], axis=1)
            inside = (row >= 0) & (row < STRETCH)
            cache_out[b] = jnp.where(inside, fresh, cache[b].astype(F32)).astype(BF16)

        return carry

    lax.fori_loop(0, blocks, place_block, 0)

    def group(g, carry):
        request = g * CHUNK // SPAN
        filled = lens[request]
        peak[...] = jnp.full_like(peak, mask_fill)
        mass[...] = jnp.zeros_like(mass)
        accum[...] = jnp.zeros_like(accum)

        def visit(b, inner):
            slot = slots[b]
            first = slot % MAXB * BS

            @pl.when((slot // MAXB == request) & (first < filled))
            def _():
                keys = cache[b][:, :HD]
                values = vt[b]
                row = lax.broadcasted_iota(jnp.int32, (BS, GROUP * TOK_DEV), 0)
                seen = row < filled - first
                for c in range(CHUNK):
                    s = g * CHUNK + c
                    query = jnp.concatenate(
                        [buf[0, slot_in(orders[0], me, s)], buf[1, slot_in(orders[1], me, s)]],
                        axis=1,
                    )
                    scores = jnp.dot(keys, query, preferred_element_type=F32)
                    scores = jnp.where(seen, scores, mask_fill)
                    old = peak[c]
                    new = jnp.maximum(old, jnp.max(scores, axis=0, keepdims=True))
                    weights = jnp.exp(scores - new)
                    retain = jnp.exp(old - new)
                    peak[c] = new
                    mass[c] = mass[c] * retain + jnp.sum(weights, axis=0, keepdims=True)
                    accum[c] = accum[c] * retain + jnp.dot(
                        values, weights.astype(BF16), preferred_element_type=F32
                    )

            return inner

        lax.fori_loop(0, blocks, visit, 0)
        for c in range(CHUNK):
            s = g * CHUNK + c
            a = accum[c]
            acc_out[s] = jnp.concatenate([a[:, :TOK_DEV], a[:, TOK_DEV:]], axis=0).astype(BF16)
            m, l = peak[c], mass[c]
            stat_out[s] = jnp.concatenate(
                [
                    m[:, :TOK_DEV],
                    m[:, TOK_DEV:],
                    l[:, :TOK_DEV],
                    l[:, TOK_DEV:],
                    gates[s],
                    jnp.zeros((3, TOK_DEV), F32),
                ],
                axis=0,
            )
        return carry

    lax.fori_loop(0, seq_count // CHUNK, group, 0)


def tail_kernel(
    bits,
    tp_count,
    acc,
    stat,
    buf,
    own_hidden,
    w_out,
    gain,
    w_gate,
    w_up,
    w_down,
    out,
    racc,
    rstat,
    full,
    part_out,
    part_in,
    residual,
    *rest,
):
    me, tp = lax.axis_index("seq"), lax.axis_index("tp")
    seq_count = 1 << bits
    rows = own_hidden.shape[0]
    parts = row_parts(rows)
    count = len(parts)
    xs, ys, zs = rest[:count], rest[count : 2 * count], rest[2 * count : 3 * count]
    acc_send, acc_recv, st_send, st_recv, tp_send, tp_recv, ag_send, ag_recv, rs_send, rs_recv = (
        rest[3 * count :]
    )
    barrier = pltpu.get_barrier_semaphore()
    for rel in range(1, seq_count):
        pl.semaphore_signal(
            barrier, inc=1, device_id=(flip(me, rel, bits), tp), device_id_type=MESH
        )
    for turn in range(1, tp_count):
        pl.semaphore_signal(
            barrier, inc=1, device_id=(me, (tp + turn) % tp_count), device_id_type=MESH
        )
    pl.semaphore_wait(barrier, seq_count - 1 + tp_count - 1)
    copies = []
    for rel in range(seq_count - 1, 0, -1):
        dest = flip(me, rel, bits)
        for src, dst, send, recv in (
            (stat, rstat, st_send, st_recv),
            (acc, racc, acc_send, acc_recv),
        ):
            copy = pltpu.make_async_remote_copy(
                src_ref=src.at[dest],
                dst_ref=dst.at[rel],
                send_sem=send.at[rel],
                recv_sem=recv.at[rel],
                device_id=(dest, tp),
                device_id_type=MESH,
            )
            copy.start()
            copies.append(copy)
    racc[0] = acc[me]
    rstat[0] = stat[me]
    orders = bit_orders(bits, 4)
    local = me % SPAN
    base = me - local
    query = jnp.concatenate([buf[0, 0], buf[1, 0]], axis=1)
    width = GROUP * TOK_DEV
    key_row = lax.broadcasted_iota(jnp.int32, (TOK_DEV, width), 0)
    query_col = lax.broadcasted_iota(jnp.int32, (TOK_DEV, width), 1) % TOK_DEV

    def own(j, states):
        old, mass, accum = states
        keys = buf[2, slot_in(orders[2], me, base + j)]
        values = buf[3, slot_in(orders[3], me, base + j)]
        scores = lax.dot_general(
            keys, query, (((0,), (0,)), ((), ())), preferred_element_type=F32
        )
        scores = jnp.where(key_row + (j - local) * TOK_DEV <= query_col, scores, mask_fill)
        new = jnp.maximum(old, jnp.max(scores, axis=0, keepdims=True))
        weights = jnp.exp(scores - new)
        retain = jnp.exp(old - new)
        mass = mass * retain + jnp.sum(weights, axis=0, keepdims=True)
        accum = accum * retain + jnp.dot(
            values, weights.astype(BF16), preferred_element_type=F32
        )
        return new, mass, accum

    self_peak, self_mass, self_accum = lax.fori_loop(
        0,
        local + 1,
        own,
        (
            jnp.full((1, width), mask_fill, F32),
            jnp.zeros((1, width), F32),
            jnp.zeros((HD, width), F32),
        ),
    )
    for copy in copies:
        copy.wait_recv()
    heads = []
    for head in range(GROUP):
        lanes = slice(head * TOK_DEV, (head + 1) * TOK_DEV)
        top = self_peak[:, lanes]
        for rel in range(seq_count):
            top = jnp.maximum(top, rstat[rel, head : head + 1, :])
        share = jnp.exp(self_peak[:, lanes] - top)
        denom = self_mass[:, lanes] * share
        total = self_accum[:, lanes] * share
        for rel in range(seq_count):
            share = jnp.exp(rstat[rel, head : head + 1, :] - top)
            denom += rstat[rel, GROUP + head : GROUP + head + 1, :] * share
            total += racc[rel, head * HD : (head + 1) * HD, :].astype(F32) * share
        heads.append(total / denom)
    attention = jnp.concatenate(heads, axis=0).T.astype(BF16)
    product = jnp.dot(attention, w_out[...], preferred_element_type=F32)
    for turn in range(tp_count):
        piece = product[turn * rows : (turn + 1) * rows]
        full[turn] = piece
        part_out[turn] = piece.astype(BF16)
    swaps = []
    for turn in range(1, tp_count):
        peer = (tp + turn) % tp_count
        copy = pltpu.make_async_remote_copy(
            src_ref=part_out.at[peer],
            dst_ref=part_in.at[turn - 1],
            send_sem=tp_send.at[turn - 1],
            recv_sem=tp_recv.at[turn - 1],
            device_id=(me, peer),
            device_id_type=MESH,
        )
        copy.start()
        swaps.append(copy)
    gate_cols = rstat[:, :, :128].reshape(seq_count * 8, 128).T
    head_total = full[tp]
    for turn in range(1, tp_count):
        swaps[turn - 1].wait_recv()
        head_total += part_in[turn - 1].astype(F32)
    rounded = (own_hidden[...].astype(F32) + head_total).astype(BF16)
    residual[...] = rounded
    normed = scaled(rounded.astype(F32), gain[...])
    for part, (start, size) in enumerate(parts):
        xs[part][pl.ds(0, size), :] = normed[start : start + size]
    walks = bit_orders(bits, count)

    def experts(part, low, high):
        start, size = parts[part]
        span = pl.ds(low * size, (high - low) * size)
        x = xs[part][span, :]
        gate_part = jnp.dot(x, w_gate[...], preferred_element_type=F32)
        up_part = jnp.dot(x, w_up[...], preferred_element_type=F32)
        inner = (gate_part / (1.0 + jnp.exp(-gate_part)) * up_part).astype(BF16)
        answer = jnp.dot(inner, w_down[...], preferred_element_type=F32).astype(BF16)
        weight = jnp.concatenate(
            [
                gate_cols[start : start + size, col : col + 1]
                for col in (8 * rel_of(walks[part], slot) + 4 for slot in range(low, high))
            ],
            axis=0,
        )
        ys[part][span, :] = (answer.astype(F32) * weight).astype(BF16)

    gathers, sums = {}, {}
    for step in range(bits):
        for part, (start, size) in enumerate(parts):
            if step:
                gathers[part, step - 1].wait_recv()
            extent = size << step
            copy = pltpu.make_async_remote_copy(
                src_ref=xs[part].at[pl.ds(0, extent), :],
                dst_ref=xs[part].at[pl.ds(extent, extent), :],
                send_sem=ag_send.at[part, step],
                recv_sem=ag_recv.at[part, step],
                device_id=(flip(me, 1 << walks[part][step], bits), tp),
                device_id_type=MESH,
            )
            copy.start()
            gathers[part, step] = copy
        if step >= 2:
            for part in range(count):
                experts(part, 0 if step == 2 else 1 << (step - 1), 1 << step)

    def send_sum(part, step):
        extent = parts[part][1] << step
        copy = pltpu.make_async_remote_copy(
            src_ref=ys[part].at[pl.ds(extent, extent), :],
            dst_ref=zs[part].at[pl.ds(extent, extent), :],
            send_sem=rs_send.at[part, step],
            recv_sem=rs_recv.at[part, step],
            device_id=(flip(me, 1 << walks[part][step], bits), tp),
            device_id_type=MESH,
        )
        copy.start()
        sums[part, step] = copy

    for part in range(count):
        gathers[part, bits - 1].wait_recv()
        experts(part, seq_count // 2, seq_count)
        send_sum(part, bits - 1)

    def arrived(part, step, low, high):
        extent = parts[part][1] << step
        mine = ys[part][pl.ds(low, high - low), :].astype(F32)
        return mine + zs[part][pl.ds(extent + low, high - low), :].astype(F32)

    for step in range(bits - 1, 0, -1):
        for part, (start, size) in enumerate(parts):
            extent = size << step
            half = extent // 2
            sums[part, step].wait_recv()
            ys[part][pl.ds(half, half), :] = arrived(part, step, half, extent).astype(BF16)
            send_sum(part, step - 1)
        for part, (start, size) in enumerate(parts):
            half = (size << step) // 2
            ys[part][pl.ds(0, half), :] = arrived(part, step, 0, half).astype(BF16)
    for part, (start, size) in enumerate(parts):
        sums[part, 0].wait_recv()
        total = arrived(part, 0, 0, size)
        out[pl.ds(start, size), :] = (
            residual[pl.ds(start, size), :].astype(F32) + total
        ).astype(BF16)
    for copy in copies + swaps + list(gathers.values()) + list(sums.values()):
        copy.wait_send()


def on_device(
    hidden,
    norm1_gain,
    w_query,
    w_key,
    w_value,
    w_out,
    norm2_gain,
    w_gate,
    w_up,
    w_down,
    cache_in,
    cache_len,
    block_table,
    routes,
    gate_w,
):
    seq_count = lax.axis_size("seq")
    tp_count = lax.axis_size("tp")
    bits = seq_count.bit_length() - 1
    seq_place = lax.axis_index("seq")
    tp_place = lax.axis_index("tp")
    vmem = pl.BlockSpec(memory_space=pltpu.VMEM)
    smem = pl.BlockSpec(memory_space=pltpu.SMEM)
    request = seq_place * TOK_DEV // STRETCH
    token = seq_place * TOK_DEV % STRETCH + jnp.arange(TOK_DEV, dtype=jnp.int32)
    positions = cache_len[request] + token
    counter = jnp.arange(HD // 2, dtype=jnp.int32).astype(F32)
    frequency = jnp.exp(counter * (-2.0 * math.log(rope_base) / HD))
    angles = positions.astype(F32)[None, :] * frequency[:, None]
    w_kv = jnp.concatenate([w_key, w_value], axis=1)
    dma = pltpu.SemaphoreType.DMA
    buf = pl.pallas_call(
        functools.partial(project_kernel, bits),
        out_shape=jax.ShapeDtypeStruct((4, seq_count, HD, TOK_DEV), BF16),
        in_specs=[vmem] * 6,
        out_specs=vmem,
        scratch_shapes=[dma((4, bits)), dma((4, bits))],
        compiler_params=pltpu.CompilerParams(
            collective_id=0, has_side_effects=True, vmem_limit_bytes=32 << 20
        ),
        name="project",
    )(hidden, norm1_gain[None, :], w_query, w_kv, jnp.cos(angles), jnp.sin(angles))

    blocks = cache_in.shape[0]
    pool_ids = seq_place * blocks + jnp.arange(blocks, dtype=jnp.int32)
    places = jnp.arange(block_table.shape[0], dtype=jnp.int32)
    slots = jnp.sum(
        jnp.where(block_table[None, :] == pool_ids[:, None], places[None, :], 0), axis=1
    )
    rows = TOK_DEV // tp_count
    experts = jnp.arange(seq_count, dtype=jnp.int32)
    gates = jnp.sum(
        jnp.where(routes.T[None] == experts[:, None, None], gate_w.T[None], 0.0), axis=1
    )
    gates = jnp.pad(gates, ((0, 0), (0, TOK_DEV - rows)))[:, None, :]
    width = GROUP * TOK_DEV
    acc, stat, cache_out = pl.pallas_call(
        functools.partial(cache_kernel, bits),
        out_shape=(
            jax.ShapeDtypeStruct((seq_count, GROUP * HD, TOK_DEV), BF16),
            jax.ShapeDtypeStruct((seq_count, 8, TOK_DEV), F32),
            jax.ShapeDtypeStruct((blocks, BS, 2 * HD), BF16),
        ),
        in_specs=[smem, smem, vmem, vmem, vmem],
        out_specs=(vmem, vmem, vmem),
        scratch_shapes=[
            pltpu.VMEM((blocks, HD, BS), BF16),
            pltpu.VMEM((CHUNK, 1, width), F32),
            pltpu.VMEM((CHUNK, 1, width), F32),
            pltpu.VMEM((CHUNK, HD, width), F32),
        ],
        compiler_params=pltpu.CompilerParams(vmem_limit_bytes=40 << 20),
        name="cached",
    )(slots, cache_len, buf, cache_in.reshape(blocks, BS, 2 * HD), gates)

    own_hidden = lax.dynamic_slice_in_dim(hidden, tp_place * rows, rows, 0)
    parts = row_parts(rows)
    held = [pltpu.VMEM((seq_count * size, D), BF16) for _, size in parts]
    count = len(parts)
    hidden_out = pl.pallas_call(
        functools.partial(tail_kernel, bits, tp_count),
        out_shape=jax.ShapeDtypeStruct((rows, D), BF16),
        in_specs=[vmem] * 9,
        out_specs=vmem,
        scratch_shapes=[
            pltpu.VMEM((seq_count, GROUP * HD, TOK_DEV), BF16),
            pltpu.VMEM((seq_count, 8, TOK_DEV), F32),
            pltpu.VMEM((tp_count, rows, D), F32),
            pltpu.VMEM((tp_count, rows, D), BF16),
            pltpu.VMEM((tp_count - 1, rows, D), BF16),
            pltpu.VMEM((rows, D), BF16),
            *held,
            *held,
            *held,
            *[dma((seq_count,))] * 4,
            *[dma((tp_count - 1,))] * 2,
            *[dma((count, bits))] * 4,
        ],
        compiler_params=pltpu.CompilerParams(
            collective_id=1, has_side_effects=True, vmem_limit_bytes=52 << 20
        ),
        name="tail",
    )(
        acc,
        stat,
        buf,
        own_hidden,
        w_out,
        norm2_gain[None, :],
        w_gate[0],
        w_up[0],
        w_down[0],
    )
    return hidden_out, cache_out[:, :, None, :]


def solution(mesh):
    placed = (
        P("seq", None),
        P(),
        P(None, "tp"),
        P(None, "tp"),
        P(None, "tp"),
        P("tp", None),
        P(),
        P("seq", None, None),
        P("seq", None, None),
        P("seq", None, None),
        P("seq", None, "tp", None),
        P(),
        P(),
        P(("seq", "tp"), None),
        P(("seq", "tp"), None),
    )
    return jax.shard_map(
        on_device,
        mesh=mesh,
        in_specs=placed,
        out_specs=(P(("seq", "tp"), None), P("seq", None, "tp", None)),
        check_vma=False,
    )
```

time: 598 us -> 184 us (0.31); the launches traced: 586 us -> 186 us
  waiting for transfers between devices: 182 us -> 0 us
  Pallas kernels: 0 us -> 177 us
  local copies, waits for them, and re-layouts: 111 us -> 5.19 us
  other arithmetic: 78.1 us -> 2.6 us
  blocking collectives: 75.3 us -> 0 us
  matrix products: 75.1 us -> 0 us
  loops' own time: 31.2 us -> 0 us
  starting transfers between devices: 19.8 us -> 0 us
  between operations: 14.3 us -> 0.84 us
    pallas_call x0 -> x3, Pallas kernels: none -> 177 us  [the longest x1 121 us: on_device(): pl.pallas_call(functools.partial(tail_kernel, bits, tp_count), out_shape=...]
    all_gather x2 -> x0, waiting for transfers between devices: 123 us -> none  [the longest x1 66.4 us: on_device(): lax.all_gather(new_rows, 'seq', axis=0, tiled=True)]
    all_to_all x1 -> x0, blocking collectives: 75.3 us -> none  [on_device(): lax.all_to_all(outgoing, 'seq', split_axis=0, concat_axis=0, tiled=True)]
    dot_general x26 -> x0, matrix products: 75.1 us -> none  [the longest x9 28 us: update(): jnp.einsum('qk,kd->qd', weights.astype(jnp.bfloat16), entries[:, HD:], pr...]
    all_to_all x4 -> x0, waiting for transfers between devices: 58.6 us -> none  [the longest x1 51.6 us: on_device(): lax.all_to_all(answered, 'seq', split_axis=0, concat_axis=0, tiled=True)]
    reduce_sum x17 -> x2, other arithmetic: 39.6 us -> 1.6 us  [the longest x1 0.86 us: on_device(): jnp.sum(jnp.where(block_table[None, :] == pool_ids[:, None], places[None,...]
    another operation x1 -> x0, loops' own time: 31.2 us -> none  [on_device(): lax.fori_loop(0, blk_count, visit_block, start_states)]
    dynamic_slice x45 -> x2, local copies, waits for them, and re-layouts: 29.1 us -> 2.28 us  [the longest x1 1.3 us: on_device(): positions = cache_len[request] + token]
  transfers between devices with their start and end apart: 7 -> 0, of which waited for: 4 -> 0; matrix products, arithmetic and copies ran while one was open for 10% -> 0% of each run, Pallas kernels for 0% -> 0%
where the time goes in v1:
time: 184 us; the launch traced here: 186 us
  Pallas kernels  177 us (96%)
  local copies, waits for them, and re-layouts  5.19 us (3%)
  other arithmetic  2.6 us (1%)
    pallas_call x1, Pallas kernels, on_device(): pl.pallas_call(functools.partial(tail_kernel, bits, tp_count), out_shape=...  121 us
    pallas_call x1, Pallas kernels, on_device(): pl.pallas_call(functools.partial(project_kernel, bits), out_shape=jax.Sha...  29 us
    pallas_call x1, Pallas kernels, on_device(): pl.pallas_call(functools.partial(cache_kernel, bits), out_shape=(jax.Shap...  27 us

profile of v1, /device:TPU:0, one launch (start us, length us, event | category | flops | bytes accessed | tf_op | source)
XLA Modules:
  0.0 185.7 jit_solution(10579882794560941393)
XLA Ops:
  0.6 0.0 copy-start.1
  0.6 0.0 copy-start.3
  0.7 0.0 copy-start.5
  0.7 1.3 dynamic_slice.6
  2.0 0.6 add_convert_fusion
  2.7 0.9 select_reduce_fusion.1.slots
  3.5 0.7 select_reduce_fusion
  4.3 0.2 multiply_sine_fusion
  4.5 1.0 constant_dynamic-slice_fusion.own_hidden
  5.5 1.1 copy.20
  6.6 1.1 copy.21
  7.6 0.0 copy-start.2
  7.7 0.0 copy-start.7
  7.7 0.1 pad_maximum_fusion.wkv
  7.8 0.0 copy-done.1
  7.8 0.0 copy-done.3
  7.8 0.0 copy-done.5
  7.9 29.0 %project.1.buf = bf16[4,16,64,256]{3,2,1,0:T(8,128)(2,1)S(1)} custom-call(bf16[256,1024]{1,0:T(8,128)(2,1)S(1)} %copy-done.1, f32[1,1024]{1,0:T(1,128)S(1)} %bitcast.13, bf16[1024,128]{1,0:T(8,128)(2,1)S(1)} %copy-done.3, bf16[1024,128]{1,0:T(8,128)(2,1)S(1)} %pad_maximum_fusion.wkv, f32[32,256]{1,0:T(8,128)S(1)} %get-tuple-element.13.cosine, ...), custom_call_target="tpu_custom_call" | custom-call | tf_op jit(solution)/shard_map/project/pallas_call | solution.py:472
  36.9 0.0 copy-done.2
  36.9 0.0 copy-done.7
  36.9 0.0 copy-start
  36.9 0.0 copy-start.4
  36.9 0.0 copy-start.6
  36.9 27.0 %cached.1 = (bf16[16,128,256]{2,1,0:T(8,128)(2,1)S(1)}, f32[16,8,256]{2,1,0:T(8,128)S(1)}, bf16[9,256,128]{2,1,0:T(8,128)(2,1)}) custom-call(s32[9]{0:T(128)S(1)} %select_reduce_fusion.1.slots, s32[2]{0:T(128)S(1)} %copy-done.7, bf16[4,16,64,256]{3,2,1,0:T(8,128)(2,1)S(1)} %project.1.buf, bf16[9,256,128]{2,1,0:T(8,128)(2,1)S(1)} %bitcast.12, ...), custom_call_target="tpu_custom_call" | custom-call | tf_op jit(solution)/shard_map/cached/pallas_call | solution.py:497
  63.9 0.0 copy-done
  63.9 0.0 copy-done.4
  63.9 0.0 copy-done.6
  64.0 121.0 %tail.1 = bf16[128,1024]{1,0:T(8,128)(2,1)S(1)} custom-call(bf16[16,128,256]{2,1,0:T(8,128)(2,1)S(1)} %get-tuple-element.5.acc, f32[16,8,256]{2,1,0:T(8,128)S(1)} %get-tuple-element.6.stat, bf16[4,16,64,256]{3,2,1,0:T(8,128)(2,1)} %copy-done, bf16[128,1024]{1,0:T(8,128)(2,1)S(1)} %constant_dynamic-slice_fusion.own_hidden, bf16[128,1024]{1,0:T(8,128)(2,1)S(1)} %copy-done.4, ...), custom_call_target="tpu_custom_call" | custom-call | tf_op jit(solution)/shard_map/tail/pallas_call | solution.py:520
  185.0 0.7 copy.24
  (4 shorter events, 0.0 us)
Async XLA Ops:
  0.6 7.2 %copy-start.1 = (bf16[256,1024]{1,0:T(8,128)(2,1)S(1)}, bf16[256,1024]{1,0:T(8,128)(2,1)}, u32[]{:S(2)}) copy-start(bf16[256,1024]{1,0:T(8,128)(2,1)} %hidden.1) | copy-start | bytes 1572868
  0.6 7.2 %copy-start.3 = (bf16[1024,128]{1,0:T(8,128)(2,1)S(1)}, bf16[1024,128]{1,0:T(8,128)(2,1)}, u32[]{:S(2)}) copy-start(bf16[1024,128]{1,0:T(8,128)(2,1)} %wq.1) | copy-start | bytes 786436
  0.7 7.2 %copy-start.5 = (f32[1024]{0:T(1024)S(1)}, f32[1024]{0:T(1024)}, u32[]{:S(2)}) copy-start(f32[1024]{0:T(1024)} %param.16) | copy-start | bytes 12292
  7.6 29.2 %copy-start.2 = (bf16[9,256,1,128]{3,1,2,0:T(8,128)(2,1)S(1)}, bf16[9,256,1,128]{3,1,2,0:T(8,128)(2,1)}, u32[]{:S(2)}) copy-start(bf16[9,256,1,128]{3,1,2,0:T(8,128)(2,1)} %param.25) | copy-start | bytes 1769476
  7.7 29.2 %copy-start.7 = (s32[2]{0:T(128)S(1)}, s32[2]{0:T(128)}, u32[]{:S(2)}) copy-start(s32[2]{0:T(128)} %lens.1) | copy-start | bytes 28
  36.9 27.1 %copy-start = (bf16[4,16,64,256]{3,2,1,0:T(8,128)(2,1)}, bf16[4,16,64,256]{3,2,1,0:T(8,128)(2,1)S(1)}, u32[]{:S(2)}) copy-start(bf16[4,16,64,256]{3,2,1,0:T(8,128)(2,1)S(1)} %project.1.buf) | copy-start | bytes 6291460
  36.9 27.1 %copy-start.4 = (bf16[128,1024]{1,0:T(8,128)(2,1)S(1)}, bf16[128,1024]{1,0:T(8,128)(2,1)}, u32[]{:S(2)}) copy-start(bf16[128,1024]{1,0:T(8,128)(2,1)} %w_out.1) | copy-start | bytes 786436
  36.9 27.1 %copy-start.6 = (f32[1024]{0:T(1024)S(1)}, f32[1024]{0:T(1024)}, u32[]{:S(2)}) copy-start(f32[1024]{0:T(1024)} %param.21) | copy-start | bytes 12292
